TPU v7x, 1024 devices: a whole 8x8x8 slice. The times are simulated.
1024 devices in a mesh: rep: 4 (over z_hi, core), fsdp: 256 (over x, y, z_lo).
Axes of the slice: x: 8, y: 8, z: 8 (z_hi: 2, z_lo: 4; z = z_hi * 4 + z_lo), core: 2. Of those that a mesh axis runs over, the one named last changes fastest.
Arguments:
- tokens: bfloat16 [4, 32768, 8192], P('rep', 'fsdp'), may hold values from -6 to 6
- local_weights: bfloat16 [4, 10, 256, 8192], P('rep', None, 'fsdp'), may hold values from -6 to 6
- base_weights: bfloat16 [10, 256, 8192], P(None, 'fsdp'), may hold values from -6 to 6
- momentum: float32 [10, 256, 8192], P(None, 'fsdp'), may hold values from -6 to 6
Outputs:
- projected: bfloat16 [4, 32768, 256], P('rep', 'fsdp')
- new_base: bfloat16 [10, 256, 8192], P(None, 'fsdp')
- new_momentum: float32 [10, 256, 8192], P(None, 'fsdp')
- new_local: bfloat16 [4, 10, 256, 8192], P('rep', None, 'fsdp')
All inputs are finite; a program needn't handle non-finite values.
Results may differ from a plain program's by a relative error of at most 0.02.
Values may be sent and summed in bfloat16 or wider, within the bound.
A program may use at most 64 MiB of HBM per device.

v0:
```python
import math

import jax
import jax.numpy as jnp
from jax import lax
from jax.sharding import PartitionSpec as P

D = 8192


def on_device(tokens, local_weights, base_weights, momentum):
    own_rows = local_weights[0]
    activations = tokens[0]
    factor = 1.0 / math.sqrt(D)
    inner_out = (
        lax.dot_general(
            activations,
            lax.all_gather(own_rows[0], "fsdp", axis=0, tiled=True),
            (((1,), (1,)), ((), ())),
            preferred_element_type=jnp.float32,
        )
        * factor
    )
    projected = inner_out.astype(jnp.bfloat16)[None]
    base_wide = base_weights.astype(jnp.float32)
    coded_delta = (base_wide - own_rows.astype(jnp.float32)).astype(jnp.bfloat16)
    replicas = lax.axis_size("rep")
    widened = lax.optimization_barrier(coded_delta).astype(jnp.float32)
    average = lax.psum(widened.astype(jnp.bfloat16), "rep").astype(jnp.float32) / replicas
    outer_grad = average.astype(jnp.bfloat16)
    outer_wide = lax.optimization_barrier(outer_grad).astype(jnp.float32)
    new_momentum = 0.9 * momentum + outer_wide
    new_base = (base_wide - 0.7 * (outer_wide + 0.9 * new_momentum)).astype(jnp.bfloat16)
    base_again = lax.optimization_barrier(new_base).astype(jnp.float32)
    new_local = (0.5 * local_weights.astype(jnp.float32) + 0.5 * base_again[None]).astype(
        jnp.bfloat16
    )
    return (projected, new_base, new_momentum, new_local)


def solution(mesh):
    return jax.shard_map(
        on_device,
        mesh=mesh,
        in_specs=(
            P("rep", "fsdp", None),
            P("rep", None, "fsdp", None),
            P(None, "fsdp", None),
            P(None, "fsdp", None),
        ),
        out_specs=(
            P("rep", "fsdp", None),
            P(None, "fsdp", None),
            P(None, "fsdp", None),
            P("rep", None, "fsdp", None),
        ),
        check_vma=False,
    )
```

profile of v0, /device:TPU:8, one launch (start us, length us, event | category | flops | bytes accessed | tf_op | source)
XLA Modules:
  0.0 1423.4 jit_solution(2987680280211838199)
XLA Ops:
  8.0 0.0 copy-start
  8.0 0.0 copy-start.1
  8.0 0.0 all-reduce.2.cloned.1.call-start
  8.1 2.0 fusion.19
  10.0 0.0 all-reduce.2.cloned.1.call-update
  10.1 0.0 all-gather.3.cloned.1.call-start
  10.1 1.5 slice_bitcast_fusion
  11.6 0.0 all-gather.3.cloned.1.call-update
  11.7 79.9 %all-reduce.2.cloned.1.call-done = bf16[10,1,8192]{2,0,1:T(8,128)(2,1)} async-done(((bf16[10,1,8192]{2,0,1:T(8,128)(2,1)}), bf16[10,1,8192]{2,0,1:T(8,128)(2,1)}) %all-reduce.2.cloned.1.call-update) | async-done | bytes 163856 | tf_op jit(solution)/shard_map/psum | solution.py:29
  91.6 1.0 multiply_convert_fusion
  92.6 1.3 convert_add_fusion.2
  94.0 0.0 copy-start.2
  94.0 1.1 copy.15
  95.0 0.0 copy-done.1
  95.0 0.8 fusion.23
  95.8 1311.4 %all-gather.3.cloned.1.call-done = bf16[256,1,1,8192]{3,2,1,0:T(2,128)(2,1)} async-done(((bf16[1,1,1,8192]{3,2,1,0:T(2,128)(2,1)}), bf16[256,1,1,8192]{3,2,1,0:T(2,128)(2,1)}) %all-gather.3.cloned.1.call-update) | async-done | bytes 4194320 | tf_op jit(solution)/shard_map/all_gather | solution.py:18
  1407.2 0.0 copy-done
  1407.2 8.7 fusion.14
  1415.9 0.0 copy-done.2
Async XLA Ops:
  8.0 1399.2 %copy-start = (bf16[1,128,8192]{2,1,0:T(8,128)(2,1)S(1)}, bf16[1,128,8192]{2,1,0:T(8,128)(2,1)}, u32[]{:S(2)}) copy-start(bf16[1,128,8192]{2,1,0:T(8,128)(2,1)} %param.4) | copy-start | bytes 6291460
  8.0 87.0 %copy-start.1 = (bf16[1,10,1,8192]{3,1,2,0:T(8,128)(2,1)S(1)}, bf16[1,10,1,8192]{3,1,2,0:T(8,128)(2,1)}, u32[]{:S(2)}) copy-start(bf16[1,10,1,8192]{3,1,2,0:T(8,128)(2,1)} %param.5) | copy-start | bytes 491524
  8.0 83.6 %all-reduce.2.cloned.1.call-start = ((), (), s32[]{:S(2)}) async-start(), calls=%async_computation | async-start | bytes 524288 | tf_op jit(solution)/shard_map/psum | solution.py:29
  10.1 1397.1 %all-gather.3.cloned.1.call-start = ((), (), s32[]{:S(2)}) async-start(), calls=%async_computation.1 | async-start | bytes 8421376 | tf_op jit(solution)/shard_map/all_gather | solution.py:18
  94.0 1322.0 %copy-start.2 = (bf16[10,1,8192]{2,0,1:T(8,128)(2,1)}, bf16[10,1,8192]{2,0,1:T(8,128)(2,1)S(1)}, u32[]{:S(2)}) copy-start(bf16[10,1,8192]{2,0,1:T(8,128)(2,1)S(1)} %get-tuple-element.17) | copy-start | bytes 491524
Sparse Core Ops, SparseCore 0:
  12.9 78.6 all-reduce.1
Sparse Core Ops, SparseCore 1:
  13.8 1393.4 all-gather.2
where the time goes:
time: 1420 us
  waiting for transfers between devices  1390 us (98%)
  between operations  15.5 us (1%)
    all_gather x1, waiting for transfers between devices, on_device(): lax.all_gather(own_rows[0], 'fsdp', axis=0, tiled=True)  1310 us
    psum x1, waiting for transfers between devices, on_device(): lax.psum(widened.astype(jnp.bfloat16), 'rep').astype(jnp.float32) / replicas  79.9 us
  transfers between devices with their start and end apart: 2, of which 2 were waited for; matrix products, arithmetic and copies ran while one was open for 0% of the time, Pallas kernels for 0%

commit v1 on v0

v1 whole, which is shorter than its diff:
```python
import functools
import math

import jax
import jax.numpy as jnp
from jax import lax
from jax.experimental import pallas as pl
from jax.experimental.pallas import tpu as pltpu
from jax.sharding import PartitionSpec as P

LANES = 128
MESH = pl.DeviceIdType.MESH
NT = (((1,), (1,)), ((), ()))


class Sizes:
    def __init__(self, x, y, z, width, layers, tokens, chunks):
        self.x, self.y, self.z = x, y, z
        self.width, self.layers, self.tokens, self.chunks = width, layers, tokens, chunks
        self.rows = x * y * z
        self.half = width // 2
        self.cols = self.half // chunks
        self.groups = self.half // LANES


def kernel(
    n,
    tok_hbm, loc_hbm, base_hbm, mom_hbm,
    proj_out, base_out, mom_out, local_out,
    tok, loc, base, mom, row, zbuf, plane, wide, ring_a, ring_b, delta, pair, cross, outer,
    load_sem, z_send, z_recv, p_send, p_recv, r_send, r_recv, d_send, d_recv,
):
    rep, me = lax.axis_index("rep"), lax.axis_index("fsdp")
    x, y, z = me // (n.y * n.z), (me // n.z) % n.y, me % n.z

    def at(x_, y_, z_):
        return {"fsdp": (x_ * n.y + y_) * n.z + z_}

    sibling = {"rep": rep + 1 - 2 * (rep % 2)}
    far = {"rep": lax.rem(rep + 2, 4)}

    def x_peer(k):
        return at(lax.rem(x + k, n.x), y, z)

    def y_peer(k):
        return at(x, lax.rem(y + k, n.y), z)

    def z_peer(k):
        return at(x, y, lax.rem(z + k, n.z))

    loads = [
        pltpu.make_async_copy(src, dst, load_sem.at[i])
        for i, (src, dst) in enumerate(((loc_hbm, loc), (base_hbm, base), (mom_hbm, mom), (tok_hbm, tok)))
    ]
    for load in loads:
        load.start()

    barrier = pltpu.get_barrier_semaphore()
    peers = (
        [sibling, far]
        + [z_peer(k) for k in range(1, n.z)]
        + [x_peer(k) for k in range(1, n.x)]
        + [y_peer(k) for k in range(1, n.y)]
    )
    for peer in peers:
        pl.semaphore_signal(barrier, inc=1, device_id=peer, device_id_type=MESH)

    def copy(src, dst, send, recv, peer):
        return pltpu.make_async_remote_copy(
            src_ref=src, dst_ref=dst, send_sem=send, recv_sem=recv, device_id=peer, device_id_type=MESH
        )

    sent = []

    def start(*args):
        c = copy(*args)
        c.start()
        sent.append(c)

    loads[0].wait()
    first = loc[0:1, :].astype(jnp.float32)
    for g in range(2 * n.groups):
        row[g : g + 1, :] = first[:, g * LANES : (g + 1) * LANES]
    for part in range(2):
        zbuf[part, z] = row[part * n.groups : (part + 1) * n.groups, :].astype(jnp.bfloat16)

    with jax.named_scope("entry_barrier"):
        pl.semaphore_wait(barrier, len(peers))

    for k in range(1, n.z):
        start(zbuf.at[:, z], zbuf.at[:, z], z_send.at[k], z_recv.at[k], z_peer(k))

    loads[1].wait()
    delta[...] = jnp.zeros_like(delta)
    delta[:, 0 : n.layers, :] = jnp.stack(
        [
            (
                base[:, h * n.half : (h + 1) * n.half].astype(jnp.float32)
                - loc[:, h * n.half : (h + 1) * n.half].astype(jnp.float32)
            ).astype(jnp.bfloat16)
            for h in range(2)
        ]
    )
    mine = rep % 2
    start(delta.at[1 - mine], pair, d_send.at[0], d_recv.at[0], sibling)

    with jax.named_scope("z_wait"):
        for k in range(1, n.z):
            slot = lax.rem(z - k + n.z, n.z)
            copy(zbuf.at[:, slot], zbuf.at[:, slot], z_send.at[k], z_recv.at[k], z_peer(k)).wait_recv()

    for k in range(1, max(n.x, n.y)):
        if k < n.x:
            start(zbuf.at[0], plane.at[0, x], p_send.at[0, k], p_recv.at[0, k], x_peer(k))
        if k < n.y:
            start(zbuf.at[1], plane.at[1, y], p_send.at[1, k], p_recv.at[1, k], y_peer(k))
    plane[0, x] = zbuf[0]
    plane[1, y] = zbuf[1]

    with jax.named_scope("pair_sum"):
        copy(pair, pair, d_send.at[0], d_recv.at[0], sibling).wait_recv()
        total = delta[mine].astype(jnp.float32) + pair[...].astype(jnp.float32)
        cross[0] = total.astype(jnp.bfloat16)
        start(cross.at[0], cross.at[1], d_send.at[1], d_recv.at[1], far)

    rings = ((ring_a, y, n.y, y_peer, x, n.x), (ring_b, x, n.x, x_peer, y, n.y))

    def block_rows(part):
        return rings[part][5] * n.z

    def hop(part, c, way, s, inward):
        ring, p, size, peer, _, _ = rings[part]
        rows = block_rows(part)
        block = lax.rem(p - (s - 1) + size, size) if way == 0 else lax.rem(p + (s - 1), size)
        got = lax.rem(p - s + size, size) if way == 0 else lax.rem(p + s, size)
        to = peer(1) if way == 0 else peer(size - 1)
        cut = pl.ds(0, rows)
        if s == size // 2:
            cut = pl.ds(0, rows // 2) if way == 0 else pl.ds(rows // 2, rows // 2)
        sems = (r_send.at[part, c, way, s - 1], r_recv.at[part, c, way, s - 1])
        slot = ring.at[c, got if inward else block, cut]
        return copy(slot, slot, *sems, to)

    def go(part, c, way, s):
        sent.append(hop(part, c, way, s, False))
        sent[-1].start()

    def arrived(part, c, way, s):
        hop(part, c, way, s, True).wait_recv()

    for part in range(2):
        ring, p, _, _, other, count = rings[part]
        with jax.named_scope("plane_wait"):
            for k in range(1, count):
                slot = lax.rem(other - k + count, count)
                copy(
                    plane.at[part, slot], plane.at[part, slot], p_send.at[part, k], p_recv.at[part, k], sibling
                ).wait_recv()
        with jax.named_scope("relayout"):
            rows = block_rows(part)
            wide[0 : rows * n.groups, :] = (
                plane[part, 0:count].reshape(rows * n.groups, LANES).astype(jnp.float32)
            )
            per = n.cols // LANES
            for c in range(n.chunks):
                for i in range(per):
                    ring[c, p, :, i * LANES : (i + 1) * LANES] = wide[
                        pl.ds(c * per + i, rows, stride=n.groups), :
                    ].astype(jnp.bfloat16)
                for way in range(2):
                    go(part, c, way, 1)

    def average():
        with jax.named_scope("average"):
            copy(cross.at[1], cross.at[1], d_send.at[1], d_recv.at[1], far).wait_recv()
            total = cross[0].astype(jnp.float32) + cross[1].astype(jnp.float32)
            outer[mine] = (total / 4.0).astype(jnp.bfloat16)
            start(outer.at[mine], outer.at[mine], d_send.at[2], d_recv.at[2], sibling)

    def update():
        with jax.named_scope("update"):
            copy(outer.at[1 - mine], outer.at[1 - mine], d_send.at[2], d_recv.at[2], sibling).wait_recv()
            loads[2].wait()
            for h in range(2):

                def one(g, _, h=h):
                    here = pl.ds(pl.multiple_of(g * LANES, LANES), LANES)
                    full = pl.ds(pl.multiple_of(h * n.half + g * LANES, LANES), LANES)
                    strided = pl.ds(h * n.groups + g, n.layers, stride=2 * n.groups)
                    grad = outer[h, 0 : n.layers, here].astype(jnp.float32)
                    moved = 0.9 * mom[strided, :] + grad
                    mom_out[strided, :] = moved
                    new_base = (base[:, full].astype(jnp.float32) - 0.7 * (grad + 0.9 * moved)).astype(jnp.bfloat16)
                    base_out[:, full] = new_base
                    local_out[:, full] = (
                        0.5 * loc[:, full].astype(jnp.float32) + 0.5 * new_base.astype(jnp.float32)
                    ).astype(jnp.bfloat16)
                    return 0

                lax.fori_loop(0, n.groups, one, 0)

    steps = (n.y // 2, n.x // 2)
    for s in range(1, max(steps)):
        with jax.named_scope("ring_step"):
            for c in range(n.chunks):
                for part in range(2):
                    if s < steps[part]:
                        for way in range(2):
                            arrived(part, c, way, s)
                            go(part, c, way, s + 1)
        if s == 1:
            average()
        if s == 2:
            update()
    if max(steps) < 2:
        average()
    if max(steps) < 3:
        update()

    loads[3].wait()
    totals = [jnp.zeros((n.tokens, n.rows), jnp.float32) for _ in range(2)]
    for c in range(n.chunks):
        for part in range(2):
            with jax.named_scope("last_wait"):
                for way in range(2):
                    arrived(part, c, way, steps[part])
            with jax.named_scope("matmul"):
                ring = rings[part][0]
                at_column = part * n.half + c * n.cols
                totals[part] += lax.dot_general(
                    tok[:, at_column : at_column + n.cols],
                    ring[c].reshape(n.rows, n.cols),
                    NT,
                    preferred_element_type=jnp.float32,
                )
    held = lax.broadcasted_iota(jnp.int32, (n.rows, n.rows), 0)
    wanted = lax.broadcasted_iota(jnp.int32, (n.rows, n.rows), 1)
    y_, x_, z_ = held // (n.x * n.z), (held // n.z) % n.x, held % n.z
    order = jnp.where((x_ * n.y + y_) * n.z + z_ == wanted, 1.0, 0.0)
    turned = jnp.dot(totals[0], order, precision=lax.Precision.HIGHEST, preferred_element_type=jnp.float32)
    proj_out[...] = ((turned + totals[1]) * (1.0 / math.sqrt(n.width))).astype(jnp.bfloat16)
    for c in sent:
        c.wait_send()


def build(n, tokens, local, base, momentum):
    bf16, f32 = jnp.bfloat16, jnp.float32
    most = max(n.x, n.y)
    dma = pltpu.SemaphoreType.DMA
    padded = -(-n.layers // 16) * 16
    return pl.pallas_call(
        functools.partial(kernel, n),
        out_shape=(
            jax.ShapeDtypeStruct((n.tokens, n.rows), bf16),
            jax.ShapeDtypeStruct((n.layers, n.width), bf16),
            jax.ShapeDtypeStruct((n.layers * n.width // LANES, LANES), f32),
            jax.ShapeDtypeStruct((n.layers, n.width), bf16),
        ),
        in_specs=[pl.BlockSpec(memory_space=pl.ANY)] * 4,
        out_specs=(pl.BlockSpec(memory_space=pltpu.VMEM),) * 4,
        scratch_shapes=[
            pltpu.VMEM((n.tokens, n.width), bf16),
            pltpu.VMEM((n.layers, n.width), bf16),
            pltpu.VMEM((n.layers, n.width), bf16),
            pltpu.VMEM((n.layers * n.width // LANES, LANES), f32),
            pltpu.VMEM((n.width // LANES, LANES), f32),
            pltpu.VMEM((2, n.z, n.groups, LANES), bf16),
            pltpu.VMEM((2, most, n.z, n.groups, LANES), bf16),
            pltpu.VMEM((most * n.z * n.groups, LANES), f32),
            pltpu.VMEM((n.chunks, n.y, n.x * n.z, n.cols), bf16),
            pltpu.VMEM((n.chunks, n.x, n.y * n.z, n.cols), bf16),
            pltpu.VMEM((2, padded, n.half), bf16),
            pltpu.VMEM((padded, n.half), bf16),
            pltpu.VMEM((2, padded, n.half), bf16),
            pltpu.VMEM((2, padded, n.half), bf16),
            dma((4,)),
            dma((n.z,)),
            dma((n.z,)),
            dma((2, most)),
            dma((2, most)),
            dma((2, n.chunks, 2, most // 2)),
            dma((2, n.chunks, 2, most // 2)),
            dma((3,)),
            dma((3,)),
        ],
        compiler_params=pltpu.CompilerParams(
            collective_id=0, has_side_effects=True, vmem_limit_bytes=40 * 1024 * 1024
        ),
    )(tokens, local, base, momentum)


def on_device(n, tokens, local_weights, base_weights, momentum):
    projected, new_base, new_momentum, new_local = build(
        n,
        tokens.reshape(n.tokens, n.width),
        local_weights.reshape(n.layers, n.width),
        base_weights.reshape(n.layers, n.width),
        momentum.reshape(n.layers * n.width // LANES, LANES),
    )
    return (
        projected[None],
        new_base.reshape(base_weights.shape),
        new_momentum.reshape(momentum.shape),
        new_local.reshape(local_weights.shape),
    )


def solution(mesh, n=Sizes(8, 8, 4, 8192, 10, 128, 4)):
    return jax.shard_map(
        functools.partial(on_device, n),
        mesh=mesh,
        in_specs=(
            P("rep", "fsdp", None),
            P("rep", None, "fsdp", None),
            P(None, "fsdp", None),
            P(None, "fsdp", None),
        ),
        out_specs=(
            P("rep", "fsdp", None),
            P(None, "fsdp", None),
            P(None, "fsdp", None),
            P("rep", None, "fsdp", None),
        ),
        check_vma=False,
    )
```

time: 1420 us -> 65.8 us (0.05)
  the two profiles are of different devices: /device:TPU:8 before, /device:TPU:6 now
where the time goes in v1:
time: 65.8 us; the launch traced here: 65.5 us
  Pallas kernels  57.6 us (88%)
  local copies, waits for them, and re-layouts  7.22 us (11%)
    pallas_call x1, Pallas kernels, build(): pl.pallas_call(functools.partial(kernel, n), out_shape=(jax.ShapeDtypeStr...  57.6 us
    unnamed x12, local copies, waits for them, and re-layouts  7.22 us

profile of v1, /device:TPU:6, one launch (start us, length us, event | category | flops | bytes accessed | tf_op | source)
XLA Modules:
  0.0 65.5 jit_solution(5439917287220004180)
XLA Ops:
  0.6 0.0 copy-start
  0.6 1.6 %copy-done = bf16[1,128,8192]{2,1,0:T(8,128)(2,1)S(1)} copy-done((bf16[1,128,8192]{2,1,0:T(8,128)(2,1)S(1)}, bf16[1,128,8192]{2,1,0:T(8,128)(2,1)}, u32[]{:S(2)}) %copy-start) | copy-done | bytes 2097176
  2.2 0.0 copy-start.1
  2.2 1.0 %copy-done.1 = f32[10,1,8192]{2,1,0:T(1,128)S(1)} copy-done((f32[10,1,8192]{2,1,0:T(1,128)S(1)}, f32[10,1,8192]{2,1,0:T(1,128)}, u32[]{:S(2)}) %copy-start.1) | copy-done | bytes 327704
  3.2 0.0 copy-start.2
  3.2 0.9 %copy-done.2 = bf16[1,10,1,8192]{3,1,2,0:T(8,128)(2,1)S(1)} copy-done((bf16[1,10,1,8192]{3,1,2,0:T(8,128)(2,1)S(1)}, bf16[1,10,1,8192]{3,1,2,0:T(8,128)(2,1)}, u32[]{:S(2)}) %copy-start.2) | copy-done | bytes 163864
  4.1 0.0 copy-start.3
  4.1 0.9 %copy-done.3 = bf16[10,1,8192]{2,0,1:T(8,128)(2,1)S(1)} copy-done((bf16[10,1,8192]{2,0,1:T(8,128)(2,1)S(1)}, bf16[10,1,8192]{2,0,1:T(8,128)(2,1)}, u32[]{:S(2)}) %copy-start.3) | copy-done | bytes 163864
  5.1 57.6 %shard_map.75 = (bf16[128,256]{1,0:T(8,128)(2,1)S(1)}, bf16[10,8192]{1,0:T(8,128)(2,1)S(1)}, f32[640,128]{1,0:T(8,128)S(1)}, bf16[10,8192]{1,0:T(8,128)(2,1)S(1)}) custom-call(bf16[128,8192]{1,0:T(8,128)(2,1)S(1)} %bitcast.8, bf16[10,8192]{1,0:T(8,128)(2,1)S(1)} %bitcast.11, bf16[10,8192]{1,0:T(8,128)(2,1)S(1)} %bitcast.12, f32[640,128]{1,0:T(8,128)S(1)} %bitcast.10), custom_call_target="tpu_custom_call" | custom-call | tf_op jit(solution)/shard_map/pallas_call | solution.py:251
  62.7 0.6 copy.14
  63.4 0.7 %copy.15 = bf16[10,1,8192]{2,0,1:T(8,128)(2,1)} copy(bf16[10,1,8192]{2,0,1:T(8,128)(2,1)S(1)} %bitcast.14) | data formatting | bytes 327680
  64.1 0.7 %copy.16 = f32[10,1,8192]{2,1,0:T(1,128)} copy(f32[10,1,8192]{2,1,0:T(1,128)S(1)} %bitcast.9) | data formatting | bytes 655360
  64.8 0.7 %copy.17 = bf16[1,10,1,8192]{3,1,2,0:T(8,128)(2,1)} copy(bf16[1,10,1,8192]{3,1,2,0:T(8,128)(2,1)S(1)} %bitcast.13) | data formatting | bytes 327680
Async XLA Ops:
  0.6 1.6 %copy-start = (bf16[1,128,8192]{2,1,0:T(8,128)(2,1)S(1)}, bf16[1,128,8192]{2,1,0:T(8,128)(2,1)}, u32[]{:S(2)}) copy-start(bf16[1,128,8192]{2,1,0:T(8,128)(2,1)} %param.4) | copy-start | bytes 6291460
  2.2 1.0 %copy-start.1 = (f32[10,1,8192]{2,1,0:T(1,128)S(1)}, f32[10,1,8192]{2,1,0:T(1,128)}, u32[]{:S(2)}) copy-start(f32[10,1,8192]{2,1,0:T(1,128)} %param.7) | copy-start | bytes 983044
  3.2 0.9 %copy-start.2 = (bf16[1,10,1,8192]{3,1,2,0:T(8,128)(2,1)S(1)}, bf16[1,10,1,8192]{3,1,2,0:T(8,128)(2,1)}, u32[]{:S(2)}) copy-start(bf16[1,10,1,8192]{3,1,2,0:T(8,128)(2,1)} %param.5) | copy-start | bytes 491524
  4.1 0.9 %copy-start.3 = (bf16[10,1,8192]{2,0,1:T(8,128)(2,1)S(1)}, bf16[10,1,8192]{2,0,1:T(8,128)(2,1)}, u32[]{:S(2)}) copy-start(bf16[10,1,8192]{2,0,1:T(8,128)(2,1)} %param.6) | copy-start | bytes 491524

commit v2 on v0

v2 whole, which is shorter than its diff:
```python
import functools
import math

import jax
import jax.numpy as jnp
from jax import lax
from jax.experimental import pallas as pl
from jax.experimental.pallas import tpu as pltpu
from jax.sharding import PartitionSpec as P

LANES = 128
MIB = 1024 * 1024
FIRST = {2: (1,), 4: (2, 1), 8: (2, 1)}
MESH = pl.DeviceIdType.MESH
NT = (((1,), (1,)), ((), ()))


class Sizes:
    def __init__(self, x, y, z, width, layers, tokens, chunks, batches=1):
        self.x, self.y, self.z = x, y, z
        self.width, self.layers, self.tokens = width, layers, tokens
        self.chunks, self.batches = chunks, batches
        self.rows = x * y * z
        self.half = width // 2
        self.part = width // 4
        self.cols = self.part // chunks
        self.groups = self.part // LANES
        self.lanes = width // LANES


def kernel(
    n,
    tok_hbm, loc_hbm, base_hbm, mom_hbm,
    proj_out, base_out, mom_out, local_out,
    tok, stage, loc, base, mom, dense, row, code, zbuf, plane, wide, ring_a, ring_b, order, give, take,
    delta, pair, cross, outer,
    load_sem, far_in, t_send, t_recv, z_send, z_recv, p_send, p_recv, r_send, r_recv, d_send, d_recv, g_send, g_recv,
):
    bf16, f32 = jnp.bfloat16, jnp.float32
    rep, me = lax.axis_index("rep"), lax.axis_index("fsdp")
    x, y, z = me // (n.y * n.z), (me // n.z) % n.y, me % n.z
    side = z % 2
    late = rep // 2
    mine = rep % 2

    def at(x_, y_, z_):
        return {"fsdp": (x_ * n.y + y_) * n.z + z_}

    sibling = {"rep": rep + 1 - 2 * mine}
    far = {"rep": lax.rem(rep + 2, 4)}
    partner = at(x, y, z + 1 - 2 * side)

    def x_peer(k):
        return at(lax.rem(x + k, n.x), y, z)

    def y_peer(k):
        return at(x, lax.rem(y + k, n.y), z)

    def z_peer(k):
        return at(x, y, lax.rem(z + k, n.z))

    loads = [
        pltpu.make_async_copy(src, dst, load_sem.at[i])
        for i, (src, dst) in enumerate(
            (
                (loc_hbm, loc),
                (base_hbm, base),
                (mom_hbm, mom),
            )
        )
    ]
    for i in range(2 * n.chunks):
        for own in range(2):
            from_ = (1 - side if own == 0 else side) * n.half + i * n.cols
            loads.append(
                pltpu.make_async_copy(
                    tok_hbm.at[:, pl.ds(pl.multiple_of(from_, n.cols), n.cols)],
                    stage.at[i] if own == 0 else tok.at[i, 0 : n.tokens],
                    load_sem.at[3 + 2 * i + own],
                )
            )
    loads[0].start()

    barrier = pltpu.get_barrier_semaphore()
    peers = (
        [sibling]
        + [z_peer(k) for k in range(1, n.z)]
        + [x_peer(k) for k in range(1, n.x)]
        + [y_peer(k) for k in range(1, n.y)]
    )
    for peer in peers:
        pl.semaphore_signal(barrier, inc=1, device_id=peer, device_id_type=MESH)

    @pl.when(late == 0)
    def _():
        pl.semaphore_signal(barrier, inc=1, device_id=far, device_id_type=MESH)

    for load in loads[1:]:
        load.start()

    def copy(src, dst, send, recv, peer):
        return pltpu.make_async_remote_copy(
            src_ref=src, dst_ref=dst, send_sem=send, recv_sem=recv, device_id=peer, device_id_type=MESH
        )

    sent = []

    def start(src, dst, send, recv, peer, listed=True):
        c = copy(src, dst, send, recv, peer)
        c.start()
        if listed:
            sent.append(c)

    def flush(left=0):
        while len(sent) > left:
            sent.pop(0).wait_send()

    loads[0].wait()
    first = loc[0:1, :].astype(f32)
    for g in range(n.lanes):
        row[g : g + 1, :] = first[:, g * LANES : (g + 1) * LANES]
    code[...] = row[...].astype(bf16).reshape(code.shape)
    zbuf[:, z] = code[side]

    pl.semaphore_wait(barrier, len(peers) + late)

    @pl.when(late == 1)
    def _():
        pl.semaphore_signal(far_in, inc=1, device_id=far, device_id_type=MESH)

    for k in range(1, n.z):
        start(code.at[lax.rem(z + k, 2)], zbuf.at[:, z], z_send.at[k], z_recv.at[k], z_peer(k))

    loads[1].wait()
    packed = n.layers * 2 * n.groups

    def lane_groups():
        for h in range(2):
            for g in range(2 * n.groups):
                at_lane = h * n.half + g * LANES
                yield slice(at_lane, at_lane + LANES), pl.ds(h * packed + g, n.layers, stride=2 * n.groups), h, g

    for here, spread, _, _ in lane_groups():
        dense[spread, :] = base[:, here].astype(f32) - loc[:, here].astype(f32)
    delta[...] = dense[...].astype(bf16).reshape(delta.shape)

    start(delta.at[1 - mine], pair, d_send.at[0], d_recv.at[0], sibling)

    def token_copy(i):
        there = tok.at[i, n.tokens : 2 * n.tokens]
        return copy(stage.at[i], there, t_send.at[i], t_recv.at[i], partner)

    token_copies = [token_copy(i) for i in range(2 * n.chunks)]
    for i in range(2 * n.chunks):
        loads[3 + 2 * i].wait()

    def send_tokens():
        for c in token_copies:
            c.start()

    pl.when(late == 0)(send_tokens)

    held = lax.broadcasted_iota(jnp.int32, (n.rows, 1), 0)
    xb, yb, zb = (size.bit_length() - 1 for size in (n.x, n.y, n.z))
    wanted = (((held >> zb) & (n.x - 1)) << (yb + zb)) | ((held >> (xb + zb)) << zb) | (held & (n.z - 1))
    spot = lax.broadcasted_iota(jnp.int32, (n.rows, n.rows), 1)
    order[...] = jnp.where(wanted == spot, 1.0, 0.0).astype(bf16)

    copy(pair, pair, d_send.at[0], d_recv.at[0], sibling).wait_recv()
    cross[0] = (delta[mine].astype(f32) + pair[...].astype(f32)).astype(bf16)

    far_copy = copy(cross.at[0], cross.at[1], d_send.at[1], d_recv.at[1], far)

    @pl.when(late == 1)
    def _():
        far_copy.start()
        send_tokens()

    for b in range(n.batches):
        deep = slice(b * n.z // n.batches, (b + 1) * n.z // n.batches)
        for slot in range(deep.start, deep.stop):

            @pl.when(z != slot)
            def _():
                k = lax.rem(z - slot + n.z, n.z)
                copy(zbuf.at[:, slot], zbuf.at[:, slot], z_send.at[k], z_recv.at[k], sibling).wait_recv()

        for k in range(1, max(n.x, n.y)):
            if k < n.x:
                start(zbuf.at[0, deep], plane.at[0, x, deep], p_send.at[0], p_recv.at[0], x_peer(k), False)
            if k < n.y:
                start(zbuf.at[1, deep], plane.at[1, y, deep], p_send.at[1], p_recv.at[1], y_peer(k), False)
    rings = ((ring_a, y, n.y, y_peer, x, n.x), (ring_b, x, n.x, x_peer, y, n.y))

    def block_rows(part):
        return rings[part][5] * n.z

    def hop(part, c, way, distance, length, inward):
        ring, p, size, peer, _, _ = rings[part]
        rows = block_rows(part)
        away = distance if inward else distance - length
        block = lax.rem(p + (size - away if way == 0 else away), size)
        cut = pl.ds(0, rows)
        if distance == size // 2:
            cut = pl.ds(0, rows // 2) if way == 0 else pl.ds(rows // 2, rows // 2)
        sems = (r_send.at[part, c, way, distance - 1], r_recv.at[part, c, way, distance - 1])
        slot = ring.at[c, block, cut]
        return copy(slot, slot, *sems, peer(length if way == 0 else size - length))

    def go(part, c, way, distance, length):
        sent.append(hop(part, c, way, distance, length, False))
        sent[-1].start()

    def arrived(part, c, way, distance):
        hop(part, c, way, distance, 1, True).wait_recv()

    for part in range(2):
        ring, p, _, _, other, count = rings[part]
        others = plane.at[part, 0 : count - 1]
        gathered = copy(others, others, p_send.at[part], p_recv.at[part], sibling)
        gathered.wait_recv()
        sent.append(gathered)
        plane[part, other] = zbuf[part]
        rows = block_rows(part)
        wide[0 : rows * n.groups, :] = plane[part, 0:count].reshape(rows * n.groups, LANES).astype(f32)
        per = n.cols // LANES
        for c in range(n.chunks):
            for i in range(per):
                ring[c, p, :, i * LANES : (i + 1) * LANES] = wide[
                    pl.ds(c * per + i, rows, stride=n.groups), :
                ].astype(bf16)
            for distance in FIRST[rings[part][2]]:
                for way in range(2):
                    go(part, c, way, distance, distance)

    @pl.when(late == 0)
    def _():
        pl.semaphore_wait(far_in, 1)
        far_copy.start()

    sent.append(far_copy)

    outer_copy = copy(outer.at[mine], outer.at[mine], d_send.at[2], d_recv.at[2], sibling)

    def average():
        copy(cross.at[1], cross.at[1], d_send.at[1], d_recv.at[1], far).wait_recv()
        outer[mine] = ((cross[0].astype(f32) + cross[1].astype(f32)) / 4.0).astype(bf16)
        outer_copy.start()

    for c in range(n.chunks):
        for part in range(2):
            if rings[part][2] == 8:
                for way in range(2):
                    arrived(part, c, way, 2)
                    go(part, c, way, 3, 1)
                    go(part, c, way, 4, 2)
    pl.when(late == 1)(average)

    for i in range(2 * n.chunks):
        loads[4 + 2 * i].wait()

    def product(part, c):
        size = rings[part][2]
        for distance in range(1, size // 2 + 1):
            if not (size == 8 and distance == 2):
                for way in range(2):
                    arrived(part, c, way, distance)
        i = part * n.chunks + c
        token_copy(i).wait_recv()
        return lax.dot_general(
            tok[i],
            rings[part][0][c].reshape(n.rows, n.cols),
            NT,
            preferred_element_type=f32,
        )

    def turn(a):
        high = a.astype(bf16)
        low = (a - high.astype(f32)).astype(bf16)
        return sum(jnp.dot(half, order[...], preferred_element_type=f32) for half in (high, low))

    first_sum = product(0, 0)
    for c in range(1, n.chunks):
        first_sum += product(0, c)
    total = turn(first_sum)
    for c in range(n.chunks):
        total += product(1, c)
    give[...] = total[n.tokens :].astype(bf16)
    start(give, take, g_send, g_recv, partner)
    pl.when(late == 0)(average)
    flush(1)
    sent.append(outer_copy)

    copy(give, take, g_send, g_recv, partner).wait_recv()
    proj_out[...] = ((total[: n.tokens] + take[...].astype(f32)) * (1.0 / math.sqrt(n.width))).astype(bf16)
    copy(outer.at[1 - mine], outer.at[1 - mine], d_send.at[2], d_recv.at[2], sibling).wait_recv()
    loads[2].wait()
    dense[...] = outer[...].reshape(dense.shape).astype(f32)
    for here, spread, h, g in lane_groups():
        strided = pl.ds(h * 2 * n.groups + g, n.layers, stride=n.lanes)
        grad = dense[spread, :]
        moved = 0.9 * mom[strided, :] + grad
        mom_out[strided, :] = moved
        new_base = (base[:, here].astype(f32) - 0.7 * (grad + 0.9 * moved)).astype(bf16)
        base_out[:, here] = new_base
        local_out[:, here] = (0.5 * loc[:, here].astype(f32) + 0.5 * new_base.astype(f32)).astype(bf16)

    flush()
    for c in token_copies:
        c.wait_send()


def build(n, tokens, local, base, momentum):
    bf16, f32 = jnp.bfloat16, jnp.float32
    most = max(n.x, n.y)
    dma = pltpu.SemaphoreType.DMA
    packed = n.layers * 2 * n.groups
    arrays = [pltpu.with_memory_space_constraint(a, pltpu.HBM) for a in (tokens, local, base, momentum)]
    return pl.pallas_call(
        functools.partial(kernel, n),
        out_shape=(
            pltpu.VMEM((n.tokens, n.rows), bf16),
            pltpu.VMEM((n.layers, n.width), bf16),
            pltpu.VMEM((n.layers * n.lanes, LANES), f32),
            pltpu.VMEM((n.layers, n.width), bf16),
        ),
        in_specs=[pl.BlockSpec(memory_space=pl.ANY)] * 4,
        out_specs=(pl.BlockSpec(memory_space=pltpu.VMEM),) * 4,
        scratch_shapes=[
            pltpu.VMEM((2 * n.chunks, 2 * n.tokens, n.cols), bf16),
            pltpu.VMEM((2 * n.chunks, n.tokens, n.cols), bf16),
            pltpu.VMEM((n.layers, n.width), bf16),
            pltpu.VMEM((n.layers, n.width), bf16),
            pltpu.VMEM((n.layers * n.lanes, LANES), f32),
            pltpu.VMEM((n.layers * n.lanes, LANES), f32),
            pltpu.VMEM((n.lanes, LANES), f32),
            pltpu.VMEM((2, 2, n.groups, LANES), bf16),
            pltpu.VMEM((2, n.z, n.groups, LANES), bf16),
            pltpu.VMEM((2, most, n.z, n.groups, LANES), bf16),
            pltpu.VMEM((most * n.z * n.groups, LANES), f32),
            pltpu.VMEM((n.chunks, n.y, n.x * n.z, n.cols), bf16),
            pltpu.VMEM((n.chunks, n.x, n.y * n.z, n.cols), bf16),
            pltpu.VMEM((n.rows, n.rows), bf16),
            pltpu.VMEM((n.tokens, n.rows), bf16),
            pltpu.VMEM((n.tokens, n.rows), bf16),
            pltpu.VMEM((2, packed, LANES), bf16),
            pltpu.VMEM((packed, LANES), bf16),
            pltpu.VMEM((2, packed, LANES), bf16),
            pltpu.VMEM((2, packed, LANES), bf16),
            dma((3 + 4 * n.chunks,)),
            pltpu.SemaphoreType.REGULAR,
            dma((2 * n.chunks,)),
            dma((2 * n.chunks,)),
            dma((n.z,)),
            dma((n.z,)),
            dma((2,)),
            dma((2,)),
            dma((2, n.chunks, 2, most // 2)),
            dma((2, n.chunks, 2, most // 2)),
            dma((3,)),
            dma((3,)),
            dma,
            dma,
        ],
        compiler_params=pltpu.CompilerParams(collective_id=0, has_side_effects=True, vmem_limit_bytes=40 * MIB),
    )(*arrays)


def store_kernel(*refs):
    copies = [pltpu.make_async_copy(refs[i], refs[4 + i], refs[8].at[i]) for i in range(4)]
    for one in copies:
        one.start()
    for one in copies:
        one.wait()


def store(*arrays):
    return pl.pallas_call(
        store_kernel,
        out_shape=tuple(jax.ShapeDtypeStruct(a.shape, a.dtype) for a in arrays),
        in_specs=[pl.BlockSpec(memory_space=pltpu.VMEM)] * 4,
        out_specs=(pl.BlockSpec(memory_space=pl.ANY),) * 4,
        scratch_shapes=[pltpu.SemaphoreType.DMA((4,))],
        compiler_params=pltpu.CompilerParams(vmem_limit_bytes=8 * MIB),
    )(*arrays)


def on_device(n, tokens, local_weights, base_weights, momentum):
    projected, new_base, new_momentum, new_local = store(
        *build(
            n,
            tokens.reshape(n.tokens, n.width),
            local_weights.reshape(n.layers, n.width),
            base_weights.reshape(n.layers, n.width),
            momentum.reshape(n.layers * n.lanes, LANES),
        )
    )
    return (
        projected[None],
        new_base.reshape(base_weights.shape),
        new_momentum.reshape(momentum.shape),
        new_local.reshape(local_weights.shape),
    )


def solution(mesh, n=Sizes(8, 8, 4, 8192, 10, 128, 2)):
    return jax.shard_map(
        functools.partial(on_device, n),
        mesh=mesh,
        in_specs=(
            P("rep", "fsdp", None),
            P("rep", None, "fsdp", None),
            P(None, "fsdp", None),
            P(None, "fsdp", None),
        ),
        out_specs=(
            P("rep", "fsdp", None),
            P(None, "fsdp", None),
            P(None, "fsdp", None),
            P("rep", None, "fsdp", None),
        ),
        check_vma=False,
    )
```

time: 1420 us -> 47.7 us (0.03)
  the two profiles are of different devices: /device:TPU:8 before, /device:TPU:1 now
where the time goes in v2:
time: 47.7 us; the launch traced here: 47.3 us
  Pallas kernels  46.6 us (98%)
  between operations  0.64 us (1%)
    pallas_call x1, Pallas kernels, build(): pl.pallas_call(functools.partial(kernel, n), out_shape=(pltpu.VMEM((n.tok...  45.7 us
    pallas_call x1, Pallas kernels, store(): pl.pallas_call(store_kernel, out_shape=tuple((jax.ShapeDtypeStruct(a.shap...  0.96 us

profile of v2, /device:TPU:1, one launch (start us, length us, event | category | flops | bytes accessed | tf_op | source)
XLA Modules:
  0.0 47.3 jit_solution(12358819579153038339)
XLA Ops:
  0.6 45.7 %shard_map.75 = (bf16[128,256]{1,0:T(8,128)(2,1)S(1)}, bf16[10,8192]{1,0:T(8,128)(2,1)S(1)}, f32[640,128]{1,0:T(8,128)S(1)}, bf16[10,8192]{1,0:T(8,128)(2,1)S(1)}) custom-call(bf16[128,8192]{1,0:T(8,128)(2,1)} %bitcast.8, bf16[10,8192]{1,0:T(8,128)(2,1)} %bitcast.10, bf16[10,8192]{1,0:T(8,128)(2,1)} %bitcast.11, f32[640,128]{1,0:T(8,128)} %bitcast.9), custom_call_target="tpu_custom_call" | custom-call | tf_op jit(solution)/shard_map/pallas_call | solution.py:319
  46.3 1.0 %shard_map.76 = (bf16[128,256]{1,0:T(8,128)(2,1)}, bf16[10,8192]{1,0:T(8,128)(2,1)}, f32[640,128]{1,0:T(8,128)}, bf16[10,8192]{1,0:T(8,128)(2,1)}) custom-call(bf16[128,256]{1,0:T(8,128)(2,1)S(1)} %get-tuple-element.12.refs_0_, bf16[10,8192]{1,0:T(8,128)(2,1)S(1)} %get-tuple-element.13.refs_1_, f32[640,128]{1,0:T(8,128)S(1)} %get-tuple-element.14.refs_2_, ...), custom_call_target="tpu_custom_call" | custom-call | tf_op jit(solution)/shard_map/pallas_call | solution.py:378

commit v3 on v2

--- a/solution.py
+++ b/solution.py
@@ -185,7 +185,7 @@
                 k = lax.rem(z - slot + n.z, n.z)
                 copy(zbuf.at[:, slot], zbuf.at[:, slot], z_send.at[k], z_recv.at[k], sibling).wait_recv()
 
-        for k in range(1, max(n.x, n.y)):
+        for k in sorted(range(1, max(n.x, n.y)), key=lambda k: -min(k, max(n.x, n.y) - k)):
             if k < n.x:
                 start(zbuf.at[0, deep], plane.at[0, x, deep], p_send.at[0], p_recv.at[0], x_peer(k), False)
             if k < n.y:
@@ -254,7 +254,19 @@
                     arrived(part, c, way, 2)
                     go(part, c, way, 3, 1)
                     go(part, c, way, 4, 2)
-    pl.when(late == 1)(average)
+    average()
+    sent.append(outer_copy)
+    copy(outer.at[1 - mine], outer.at[1 - mine], d_send.at[2], d_recv.at[2], sibling).wait_recv()
+    loads[2].wait()
+    dense[...] = outer[...].reshape(dense.shape).astype(f32)
+    for here, spread, h, g in lane_groups():
+        strided = pl.ds(h * 2 * n.groups + g, n.layers, stride=n.lanes)
+        grad = dense[spread, :]
+        moved = 0.9 * mom[strided, :] + grad
+        mom_out[strided, :] = moved
+        new_base = (base[:, here].astype(f32) - 0.7 * (grad + 0.9 * moved)).astype(bf16)
+        base_out[:, here] = new_base
+        local_out[:, here] = (0.5 * loc[:, here].astype(f32) + 0.5 * new_base.astype(f32)).astype(bf16)
 
     for i in range(2 * n.chunks):
         loads[4 + 2 * i].wait()
@@ -287,24 +299,10 @@
         total += product(1, c)
     give[...] = total[n.tokens :].astype(bf16)
     start(give, take, g_send, g_recv, partner)
-    pl.when(late == 0)(average)
     flush(1)
-    sent.append(outer_copy)
 
     copy(give, take, g_send, g_recv, partner).wait_recv()
     proj_out[...] = ((total[: n.tokens] + take[...].astype(f32)) * (1.0 / math.sqrt(n.width))).astype(bf16)
-    copy(outer.at[1 - mine], outer.at[1 - mine], d_send.at[2], d_recv.at[2], sibling).wait_recv()
-    loads[2].wait()
-    dense[...] = outer[...].reshape(dense.shape).astype(f32)
-    for here, spread, h, g in lane_groups():
-        strided = pl.ds(h * 2 * n.groups + g, n.layers, stride=n.lanes)
-        grad = dense[spread, :]
-        moved = 0.9 * mom[strided, :] + grad
-        mom_out[strided, :] = moved
-        new_base = (base[:, here].astype(f32) - 0.7 * (grad + 0.9 * moved)).astype(bf16)
-        base_out[:, here] = new_base
-        local_out[:, here] = (0.5 * loc[:, here].astype(f32) + 0.5 * new_base.astype(f32)).astype(bf16)
-
     flush()
     for c in token_copies:
         c.wait_send()
@@ -403,7 +401,7 @@
     )
 
 
-def solution(mesh, n=Sizes(8, 8, 4, 8192, 10, 128, 2)):
+def solution(mesh, n=Sizes(8, 8, 4, 8192, 10, 128, 1)):
     return jax.shard_map(
         functools.partial(on_device, n),
         mesh=mesh,

time: 47.7 us -> 45.7 us (0.958)
  Pallas kernels: 46.6 us -> 44.8 us
    pallas_call x1, Pallas kernels: 45.7 us -> 43.9 us  [build(): pl.pallas_call(functools.partial(kernel, n), out_shape=(pltpu.VMEM((n.tok...]
where the time goes in v3:
time: 45.7 us; the launch traced here: 45.5 us
  Pallas kernels  44.8 us (98%)
  between operations  0.64 us (1%)
    pallas_call x1, Pallas kernels, build(): pl.pallas_call(functools.partial(kernel, n), out_shape=(pltpu.VMEM((n.tok...  43.9 us
    pallas_call x1, Pallas kernels, store(): pl.pallas_call(store_kernel, out_shape=tuple((jax.ShapeDtypeStruct(a.shap...  0.96 us

profile of v3, /device:TPU:1, one launch (start us, length us, event | category | flops | bytes accessed | tf_op | source)
XLA Modules:
  0.0 45.5 jit_solution(2261254368654745993)
XLA Ops:
  0.6 43.9 %shard_map.75 = (bf16[128,256]{1,0:T(8,128)(2,1)S(1)}, bf16[10,8192]{1,0:T(8,128)(2,1)S(1)}, f32[640,128]{1,0:T(8,128)S(1)}, bf16[10,8192]{1,0:T(8,128)(2,1)S(1)}) custom-call(bf16[128,8192]{1,0:T(8,128)(2,1)} %bitcast.8, bf16[10,8192]{1,0:T(8,128)(2,1)} %bitcast.10, bf16[10,8192]{1,0:T(8,128)(2,1)} %bitcast.11, f32[640,128]{1,0:T(8,128)} %bitcast.9), custom_call_target="tpu_custom_call" | custom-call | tf_op jit(solution)/shard_map/pallas_call | solution.py:317
  44.5 1.0 %shard_map.76 = (bf16[128,256]{1,0:T(8,128)(2,1)}, bf16[10,8192]{1,0:T(8,128)(2,1)}, f32[640,128]{1,0:T(8,128)}, bf16[10,8192]{1,0:T(8,128)(2,1)}) custom-call(bf16[128,256]{1,0:T(8,128)(2,1)S(1)} %get-tuple-element.12.refs_0_, bf16[10,8192]{1,0:T(8,128)(2,1)S(1)} %get-tuple-element.13.refs_1_, f32[640,128]{1,0:T(8,128)S(1)} %get-tuple-element.14.refs_2_, ...), custom_call_target="tpu_custom_call" | custom-call | tf_op jit(solution)/shard_map/pallas_call | solution.py:376

commit v4 on v3

--- a/solution.py
+++ b/solution.py
@@ -185,11 +185,11 @@
                 k = lax.rem(z - slot + n.z, n.z)
                 copy(zbuf.at[:, slot], zbuf.at[:, slot], z_send.at[k], z_recv.at[k], sibling).wait_recv()
 
-        for k in sorted(range(1, max(n.x, n.y)), key=lambda k: -min(k, max(n.x, n.y) - k)):
-            if k < n.x:
-                start(zbuf.at[0, deep], plane.at[0, x, deep], p_send.at[0], p_recv.at[0], x_peer(k), False)
-            if k < n.y:
-                start(zbuf.at[1, deep], plane.at[1, y, deep], p_send.at[1], p_recv.at[1], y_peer(k), False)
+        lines = ((x, n.x, x_peer), (y, n.y, y_peer))
+        for part, (place, count, peer) in enumerate(lines):
+            for k in sorted(range(1, count), key=lambda k: -min(k, count - k)):
+                to = plane.at[part, place, deep]
+                start(zbuf.at[part, deep], to, p_send.at[part], p_recv.at[part], peer(k), False)
     rings = ((ring_a, y, n.y, y_peer, x, n.x), (ring_b, x, n.x, x_peer, y, n.y))
 
     def block_rows(part):

time: 45.7 us -> 45.7 us (level)
  no operation moved by 1% of the time
where the time goes in v4:
time: 45.7 us; the launch traced here: 45.5 us
  Pallas kernels  44.8 us (98%)
  between operations  0.64 us (1%)
    pallas_call x1, Pallas kernels, build(): pl.pallas_call(functools.partial(kernel, n), out_shape=(pltpu.VMEM((n.tok...  43.9 us
    pallas_call x1, Pallas kernels, store(): pl.pallas_call(store_kernel, out_shape=tuple((jax.ShapeDtypeStruct(a.shap...  0.96 us

profile of v4, /device:TPU:1, one launch (start us, length us, event | category | flops | bytes accessed | tf_op | source)
XLA Modules:
  0.0 45.5 jit_solution(4414243997655937919)
XLA Ops:
  0.6 43.9 %shard_map.75 = (bf16[128,256]{1,0:T(8,128)(2,1)S(1)}, bf16[10,8192]{1,0:T(8,128)(2,1)S(1)}, f32[640,128]{1,0:T(8,128)S(1)}, bf16[10,8192]{1,0:T(8,128)(2,1)S(1)}) custom-call(bf16[128,8192]{1,0:T(8,128)(2,1)} %bitcast.8, bf16[10,8192]{1,0:T(8,128)(2,1)} %bitcast.10, bf16[10,8192]{1,0:T(8,128)(2,1)} %bitcast.11, f32[640,128]{1,0:T(8,128)} %bitcast.9), custom_call_target="tpu_custom_call" | custom-call | tf_op jit(solution)/shard_map/pallas_call | solution.py:317
  44.5 1.0 %shard_map.76 = (bf16[128,256]{1,0:T(8,128)(2,1)}, bf16[10,8192]{1,0:T(8,128)(2,1)}, f32[640,128]{1,0:T(8,128)}, bf16[10,8192]{1,0:T(8,128)(2,1)}) custom-call(bf16[128,256]{1,0:T(8,128)(2,1)S(1)} %get-tuple-element.12.refs_0_, bf16[10,8192]{1,0:T(8,128)(2,1)S(1)} %get-tuple-element.13.refs_1_, f32[640,128]{1,0:T(8,128)S(1)} %get-tuple-element.14.refs_2_, ...), custom_call_target="tpu_custom_call" | custom-call | tf_op jit(solution)/shard_map/pallas_call | solution.py:376
